TPU v7x, 32 devices: a whole 2x2x4 slice. The times are simulated.
32 devices in a mesh: dp: 8 (over z, x), tensor: 4 (over y, core).
Axes of the slice: x: 2, y: 2, z: 4, core: 2. Of those that a mesh axis runs over, the one named last changes fastest.
Arguments:
- attention_grads: bfloat16 [8, 1, 512, 2048], P('dp', None, None, 'tensor')
- expert_grads: bfloat16 [8, 1, 2, 512, 4096], P('dp', None, None, None, 'tensor')
- routing_grads: bfloat16 [8, 4, 1, 36, 512], P('dp', 'tensor'), may hold values from -320 to 320
- attention_master: float32 [512, 2048], P('dp', 'tensor'), may hold values from -0.25 to 0.25
- attention_first: float32 [512, 2048], P('dp', 'tensor'), may hold values from -4 to 4
- attention_second: float32 [512, 2048], P('dp', 'tensor'), may hold values from 0.05 to 2
- expert_master: float32 [2, 512, 4096], P(None, 'dp', 'tensor'), may hold values from -0.25 to 0.25
- expert_first: float32 [2, 512, 4096], P(None, 'dp', 'tensor'), may hold values from -4 to 4
- expert_second: float32 [2, 512, 4096], P(None, 'dp', 'tensor'), may hold values from 0.05 to 2
- routing_master: float32 [36, 512], P(None, ('dp', 'tensor')), may hold values from -4 to 4
- routing_first: float32 [36, 512], P(None, ('dp', 'tensor')), may hold values from -4 to 4
- routing_second: float32 [36, 512], P(None, ('dp', 'tensor')), may hold values from 0.05 to 2
- step_count: int32 [1], replicated, may hold values from 1 to 1000
- learn_rate: float32 [1], replicated, may hold values from 0.05 to 0.3
- clip_level: float32 [1], replicated, may hold values from 0.5 to 2
Outputs:
- attention_renewed: float32 [512, 2048], P('dp', 'tensor')
- attention_momentum: float32 [512, 2048], P('dp', 'tensor')
- attention_variance: float32 [512, 2048], P('dp', 'tensor')
- attention_served: bfloat16 [512, 2048], P(None, 'tensor')
- expert_renewed: float32 [2, 512, 4096], P(None, 'dp', 'tensor')
- expert_momentum: float32 [2, 512, 4096], P(None, 'dp', 'tensor')
- expert_variance: float32 [2, 512, 4096], P(None, 'dp', 'tensor')
- expert_served: bfloat16 [2, 512, 4096], P(None, None, 'tensor')
- routing_renewed: float32 [36, 512], P(None, ('dp', 'tensor'))
- routing_momentum: float32 [36, 512], P(None, ('dp', 'tensor'))
- routing_variance: float32 [36, 512], P(None, ('dp', 'tensor'))
- routing_served: bfloat16 [36, 512], replicated
Inputs may be any that keep to these rules, and one draw needn't show every extreme that they name: `step_count`: the number of optimizer steps taken, this one included.
All inputs are finite; a program needn't handle non-finite values.
Results may differ from a plain program's by a relative error of at most 0.0004.
Values may be sent and summed in bfloat16 or wider, within the bound.
A program may use at most 64 MiB of HBM per device.

v0:
```python
from functools import reduce

import jax
import jax.numpy as jnp
from jax import lax
from jax.sharding import PartitionSpec as P

EXPERTS = 32
PARAMS = 5261312


BETA_ONE = 0.9
BETA_TWO = 0.999
EPSILON = 1e-08
DECAY = 0.1


def micro_total(blocks):
    return reduce(lambda left, right: left + right, [blocks[0].astype(jnp.float32)])


def adam_update(grad_sum, master, first, second, clip, rate, first_fix, second_fix, mask):
    grad = clip * grad_sum
    momentum = BETA_ONE * first + (1.0 - BETA_ONE) * grad
    variance = BETA_TWO * second + (1.0 - BETA_TWO) * grad * grad
    update = (
        momentum / first_fix / (jnp.sqrt(variance / second_fix) + EPSILON) + DECAY * mask * master
    )
    renewed = master - rate * update
    return (renewed, momentum, variance, renewed.astype(jnp.bfloat16))


def local(
    attention_grads,
    expert_grads,
    routing_grads,
    attention_master,
    attention_first,
    attention_second,
    expert_master,
    expert_first,
    expert_second,
    routing_master,
    routing_first,
    routing_second,
    step_count,
    learn_rate,
    clip_level,
):
    attention_local = attention_grads[0]
    expert_local = expert_grads[0]
    attention_sum = lax.psum_scatter(
        micro_total(attention_local), "dp", scatter_dimension=0, tiled=True
    )
    expert_sum = lax.psum_scatter(micro_total(expert_local), "dp", scatter_dimension=1, tiled=True)
    expert_pieces = [expert_sum[index] for index in range(expert_sum.shape[0])]
    routing_local = micro_total(routing_grads[0, 0])
    routing_sum = lax.psum_scatter(routing_local, ("dp", "tensor"), scatter_dimension=1, tiled=True)
    expert_squares = reduce(
        lambda left, right: left + right, [jnp.sum(piece * piece) for piece in expert_pieces]
    )
    attention_total, expert_total, routing_total = lax.psum(
        (
            jnp.sum(attention_sum * attention_sum),
            expert_squares,
            jnp.sum(routing_sum * routing_sum),
        ),
        ("dp", "tensor"),
    )
    grad_norm = jnp.sqrt(attention_total + expert_total + routing_total)
    clip = jnp.minimum(1.0, clip_level[0] * jnp.sqrt(jnp.float32(PARAMS)) / (grad_norm + 1e-06))
    steps_done = step_count[0].astype(jnp.float32)
    first_fix = 1.0 - jnp.power(jnp.float32(BETA_ONE), steps_done)
    second_fix = 1.0 - jnp.power(jnp.float32(BETA_TWO), steps_done)
    rate = learn_rate[0]
    attention_out = adam_update(
        attention_sum,
        attention_master,
        attention_first,
        attention_second,
        clip,
        rate,
        first_fix,
        second_fix,
        jnp.float32(1.0),
    )
    attention_served = lax.all_gather(attention_out[3], "dp", axis=0, tiled=True)
    expert_sum = jnp.stack(expert_pieces, axis=0)
    expert_out = adam_update(
        expert_sum,
        expert_master,
        expert_first,
        expert_second,
        clip,
        rate,
        first_fix,
        second_fix,
        jnp.float32(1.0),
    )
    expert_renewed, expert_momentum, expert_variance = (expert_out[0], expert_out[1], expert_out[2])
    expert_served = lax.all_gather(expert_out[3], "dp", axis=1, tiled=True)
    row_index = jnp.arange(routing_master.shape[0], dtype=jnp.int32)
    routing_mask = (row_index < EXPERTS).astype(jnp.float32)[:, None]
    routing_out = adam_update(
        routing_sum,
        routing_master,
        routing_first,
        routing_second,
        clip,
        rate,
        first_fix,
        second_fix,
        routing_mask,
    )
    routing_served = lax.all_gather(routing_out[3], ("dp", "tensor"), axis=1, tiled=True)
    return (
        attention_out[0],
        attention_out[1],
        attention_out[2],
        attention_served,
        expert_renewed,
        expert_momentum,
        expert_variance,
        expert_served,
        routing_out[0],
        routing_out[1],
        routing_out[2],
        routing_served,
    )


def solution(mesh):
    in_specs = (
        P("dp", None, None, "tensor"),
        P("dp", None, None, None, "tensor"),
        P("dp", "tensor", None, None, None),
        P("dp", "tensor"),
        P("dp", "tensor"),
        P("dp", "tensor"),
        P(None, "dp", "tensor"),
        P(None, "dp", "tensor"),
        P(None, "dp", "tensor"),
        P(None, ("dp", "tensor")),
        P(None, ("dp", "tensor")),
        P(None, ("dp", "tensor")),
        P(),
        P(),
        P(),
    )
    out_specs = (
        P("dp", "tensor"),
        P("dp", "tensor"),
        P("dp", "tensor"),
        P(None, "tensor"),
        P(None, "dp", "tensor"),
        P(None, "dp", "tensor"),
        P(None, "dp", "tensor"),
        P(None, None, "tensor"),
        P(None, ("dp", "tensor")),
        P(None, ("dp", "tensor")),
        P(None, ("dp", "tensor")),
        P(),
    )
    return jax.shard_map(local, mesh=mesh, in_specs=in_specs, out_specs=out_specs, check_vma=False)
```

profile of v0, /device:TPU:0, one launch (start us, length us, event | category | flops | bytes accessed | tf_op | source)
XLA Modules:
  0.0 435.4 jit_solution(10603458051913512915)
XLA Ops:
  7.2 0.0 copy-start
  7.2 0.0 reduce-scatter.8.cloned.1.call-start
  7.2 1.1 copy.29
  8.3 0.7 bitcast_convert_fusion.2
  9.0 0.0 reduce-scatter.8.cloned.1.call-update
  9.0 0.0 reduce-scatter.4.cloned.1.call-start
  9.1 2.1 bitcast_convert_fusion.1
  11.2 0.0 reduce-scatter.4.cloned.1.call-update
  11.3 0.0 reduce-scatter.6.cloned.1.call-start
  11.3 0.0 copy-done
  11.3 2.4 bitcast_convert_fusion
  13.7 0.0 reduce-scatter.6.cloned.1.call-update
  13.8 0.0 all-gather.2.cloned.1.call-start
  15.9 131.4 %reduce-scatter.8.cloned.1.call-done = f32[36,16]{0,1:T(8,128)} async-done(((f32[36,512]{0,1:T(8,128)}), f32[36,16]{0,1:T(8,128)}) %reduce-scatter.8.cloned.1.call-update) | async-done | bytes 2320 | tf_op jit(solution)/shard_map/reduce_scatter | solution.py:58
  147.4 1.3 multiply_reduce_fusion.1
  148.7 62.3 %reduce-scatter.4.cloned.1.call-done = f32[64,512]{1,0:T(8,128)} async-done(((f32[512,512]{1,0:T(8,128)}), f32[64,512]{1,0:T(8,128)}) %reduce-scatter.4.cloned.1.call-update) | async-done | bytes 131088 | tf_op jit(solution)/shard_map/reduce_scatter | solution.py:52
  211.0 1.5 multiply_reduce_fusion
  212.6 89.1 %reduce-scatter.6.cloned.1.call-done = f32[2,64,1024]{2,1,0:T(8,128)} async-done(((f32[2,512,1024]{2,1,0:T(8,128)}), f32[2,64,1024]{2,1,0:T(8,128)}) %reduce-scatter.6.cloned.1.call-update) | async-done | bytes 524304 | tf_op jit(solution)/shard_map/reduce_scatter | solution.py:55
  301.7 1.7 fusion.1
  306.0 40.3 %psum.25 = f32[]{:T(128)} all-reduce(f32[]{:T(128)S(6)} %add.71), channel_id=1, replica_groups=mesh['dp'=8,'tensor'=4] {'dp','tensor'}, use_global_device_ids=true, to_apply=%region_2.0 | all-reduce | flops 1 | bytes 8 | tf_op jit(solution)/shard_map/psum | solution.py:62
  347.0 0.0 copy-done.1
  347.0 0.0 copy-done.2
  347.1 0.0 copy-done.3
  347.1 0.0 copy-start.4
  347.1 0.0 copy-start.5
  347.1 0.0 copy-start.6
  347.1 0.0 copy-start.7
  347.1 0.0 copy-start.8
  347.1 0.0 copy-start.9
  347.1 0.0 copy-start.10
  347.1 0.0 copy-start.11
  347.2 2.7 fusion.7
  349.8 0.0 all-gather.2.cloned.1.call-update
  349.9 0.0 copy-done.4
  349.9 0.0 copy-done.5
  349.9 0.0 copy-done.6
  349.9 0.0 copy-done.7
  349.9 0.8 fusion.9
  350.7 32.6 %all_gather.9 = bf16[512,512]{1,0:T(8,128)(2,1)S(1)} all-gather(bf16[64,512]{1,0:T(8,128)(2,1)S(1)} %get-tuple-element.34), channel_id=1, replica_groups=mesh['dp'=8,'tensor'=4] {'dp'}, dimensions={0}, use_global_device_ids=true | all-gather | bytes 589824 | tf_op jit(solution)/shard_map/all_gather | solution.py:87
  383.3 0.0 copy-done.8
  383.3 0.0 copy-done.9
  383.3 0.0 copy-done.10
  383.3 0.0 copy-done.11
  383.3 0.6 fusion.5
  383.9 40.3 %all_gather.11 = bf16[36,512]{0,1:T(8,128)(2,1)S(1)} all-gather(bf16[36,16]{0,1:T(8,128)(2,1)S(1)} %get-tuple-element.26), channel_id=1, replica_groups=mesh['dp'=8,'tensor'=4] {'dp','tensor'}, dimensions={1}, use_global_device_ids=true | all-gather | bytes 38016 | tf_op jit(solution)/shard_map/all_gather | solution.py:115
  424.2 0.7 copy.30
  425.0 0.8 copy.36
  425.8 3.1 copy.37
  (5 shorter events, 0.0 us)
Async XLA Ops:
  7.2 4.1 copy-start
  7.2 140.2 %reduce-scatter.8.cloned.1.call-start = ((), (), s32[]{:S(2)}) async-start(), calls=%async_computation.5 | async-start | bytes 270336 | tf_op jit(solution)/shard_map/reduce_scatter | solution.py:58
  9.0 202.0 %reduce-scatter.4.cloned.1.call-start = ((), (), s32[]{:S(2)}) async-start(), calls=%async_computation.3 | async-start | bytes 1179648 | tf_op jit(solution)/shard_map/reduce_scatter | solution.py:52
  11.3 290.4 %reduce-scatter.6.cloned.1.call-start = ((), (), s32[]{:S(2)}) async-start(), calls=%async_computation.4 | async-start | bytes 4718592 | tf_op jit(solution)/shard_map/reduce_scatter | solution.py:55
  13.7 333.3 %copy-start.1 = (f32[2,64,1024]{2,1,0:T(8,128)S(1)}, f32[2,64,1024]{2,1,0:T(8,128)}, u32[]{:S(2)}) copy-start(f32[2,64,1024]{2,1,0:T(8,128)} %param.21) | copy-start | bytes 1572868
  13.7 333.3 %copy-start.2 = (f32[2,64,1024]{2,1,0:T(8,128)S(1)}, f32[2,64,1024]{2,1,0:T(8,128)}, u32[]{:S(2)}) copy-start(f32[2,64,1024]{2,1,0:T(8,128)} %param.23) | copy-start | bytes 1572868
  13.7 333.3 %copy-start.3 = (f32[2,64,1024]{2,1,0:T(8,128)S(1)}, f32[2,64,1024]{2,1,0:T(8,128)}, u32[]{:S(2)}) copy-start(f32[2,64,1024]{2,1,0:T(8,128)} %param.22) | copy-start | bytes 1572868
  13.8 411.2 %all-gather.2.cloned.1.call-start = ((), (), s32[]{:S(2)}) async-start(), calls=%async_computation.6 | async-start | bytes 2359296 | tf_op jit(solution)/shard_map/all_gather | solution.py:101
  347.1 2.8 copy-start.4
  347.1 2.8 copy-start.5
  347.1 2.8 copy-start.6
  347.1 2.8 copy-start.7
  347.1 36.2 %copy-start.8 = (f32[36,16]{0,1:T(8,128)S(1)}, f32[36,16]{0,1:T(8,128)}, u32[]{:S(2)}) copy-start(f32[36,16]{0,1:T(8,128)} %reduce-scatter.8.cloned.1.call-done) | copy-start | bytes 6916
  347.1 36.2 %copy-start.9 = (f32[36,16]{0,1:T(8,128)S(1)}, f32[36,16]{0,1:T(8,128)}, u32[]{:S(2)}) copy-start(f32[36,16]{0,1:T(8,128)} %param.24) | copy-start | bytes 6916
  347.1 36.2 %copy-start.10 = (f32[36,16]{0,1:T(8,128)S(1)}, f32[36,16]{0,1:T(8,128)}, u32[]{:S(2)}) copy-start(f32[36,16]{0,1:T(8,128)} %param.26) | copy-start | bytes 6916
  347.1 36.2 %copy-start.11 = (f32[36,16]{0,1:T(8,128)S(1)}, f32[36,16]{0,1:T(8,128)}, u32[]{:S(2)}) copy-start(f32[36,16]{0,1:T(8,128)} %param.25) | copy-start | bytes 6916
Sparse Core Ops, SparseCore 0:
  10.8 136.5 reduce-scatter.7
  151.7 59.2 reduce-scatter.3
  214.7 86.9 reduce-scatter.5
  350.0 50.8 all-gather.1
where the time goes:
time: 436 us; the launch traced here: 435 us
  waiting for transfers between devices  283 us (65%)
  blocking collectives  113 us (26%)
  between operations  19.4 us (4%)
  other arithmetic  13.9 us (3%)
  local copies, waits for them, and re-layouts  5.74 us (1%)
    reduce_scatter x1, waiting for transfers between devices, local(): lax.psum_scatter(routing_local, ('dp', 'tensor'), scatter_dimension=1, ti...  131 us
    reduce_scatter x1, waiting for transfers between devices, local(): lax.psum_scatter(micro_total(expert_local), 'dp', scatter_dimension=1, ti...  89.1 us
    reduce_scatter x1, waiting for transfers between devices, local(): lax.psum_scatter(micro_total(attention_local), 'dp', scatter_dimension=0,...  62.3 us
    psum x1, blocking collectives, local(): lax.psum((jnp.sum(attention_sum * attention_sum), expert_squares, jnp.sum...  40.3 us
    all_gather x1, blocking collectives, local(): lax.all_gather(routing_out[3], ('dp', 'tensor'), axis=1, tiled=True)  40.3 us
    all_gather x1, blocking collectives, local(): lax.all_gather(attention_out[3], 'dp', axis=0, tiled=True)  32.6 us
  transfers between devices with their start and end apart: 4, of which 3 were waited for; matrix products, arithmetic and copies ran while one was open for 2% of the time, Pallas kernels for 0%

commit v1 on v0

--- a/solution.py
+++ b/solution.py
@@ -1,8 +1,12 @@
+import functools
 from functools import reduce
 
 import jax
 import jax.numpy as jnp
+import numpy as np
 from jax import lax
+from jax.experimental import pallas as pl
+from jax.experimental.pallas import tpu as pltpu
 from jax.sharding import PartitionSpec as P
 
 EXPERTS = 32
@@ -129,6 +133,538 @@
     )
 
 
+MESH = pl.DeviceIdType.MESH
+F32 = jnp.float32
+BF16 = jnp.bfloat16
+WIDE = 512
+
+
+def power(base, steps):
+    result = jnp.full((1, 1), 1.0, F32)
+    for bit in range(10):
+        factor = F32(float(np.float32(base)) ** (2**bit))
+        result = result * jnp.where((steps >> bit) & 1 == 1, factor, F32(1.0))
+    return result
+
+
+def ring_kernel(
+    n,
+    m,
+    ag,
+    eg,
+    rg,
+    am,
+    af,
+    av,
+    em,
+    ef,
+    ev,
+    rm,
+    rf,
+    rv,
+    step_ref,
+    rate_ref,
+    level_ref,
+    o_am,
+    o_af,
+    o_av,
+    o_as,
+    o_em,
+    o_ef,
+    o_ev,
+    o_es,
+    o_rm,
+    o_rf,
+    o_rv,
+    o_rs,
+    ga,
+    ge,
+    st,
+    raw_in,
+    sum_in,
+    stage,
+    gsum,
+    served,
+    squares,
+    norm_t,
+    norm_d,
+    pad,
+    route_out,
+    route_in,
+    route_t,
+    serve_t,
+    serve_d,
+    load_sem,
+    rs_send,
+    rs_recv,
+    ag_send,
+    ag_recv,
+    norm_sem,
+    route_sem,
+    out_sem,
+):
+    d = lax.axis_index("dp")
+    t = lax.axis_index("tensor")
+    half_n = n // 2
+    rows = am.shape[0]
+    hr = rows // 2
+    wa = am.shape[1]
+    ne, _, we = em.shape
+    pieces = [(None, 0, wa)] + [(e, wa + e * we, we) for e in range(ne)]
+    z, x = d // 2, d % 2
+    pos = z + x * (n - 1 - 2 * z)
+
+    def at_pos(p):
+        p = (p + 2 * n) % n
+        return 2 * p + (p // half_n) * (2 * n - 1 - 4 * p)
+
+    peers = (at_pos(pos + 1), at_pos(pos - 1))
+    sign = (1, -1)
+    length = [[half_n, half_n - 1], [half_n - 1, half_n]]
+
+    def row0(owner, h):
+        return pl.ds(pl.multiple_of(owner * rows + h * hr, hr), hr)
+
+    loads = [
+        pltpu.make_async_copy(ag.at[0, 0], ga, load_sem.at[0]),
+        pltpu.make_async_copy(eg.at[0, 0], ge, load_sem.at[1]),
+    ]
+    k = 2
+    state_loads = []
+    for which, (a, e) in enumerate(((am, em), (af, ef), (av, ev))):
+        for e_i, off, cols in pieces:
+            src = a if e_i is None else e.at[e_i]
+            state_loads.append(
+                pltpu.make_async_copy(src, st.at[which, :, off : off + cols], load_sem.at[k])
+            )
+            k += 1
+    for c in loads + state_loads:
+        c.start()
+
+    barrier = pltpu.get_barrier_semaphore()
+    for k in range(1, n):
+        pl.semaphore_signal(barrier, inc=1, device_id=((d + k) % n, t), device_id_type=MESH)
+    for k in range(1, m):
+        pl.semaphore_signal(barrier, inc=1, device_id=(d, (t + k) % m), device_id_type=MESH)
+
+    rr, rc = rg.shape[-2:]
+    own_cols = rc // (n * m)
+    blocks = rc // 128
+    per_block = 128 // own_cols
+    pad[...] = jnp.zeros_like(pad)
+    pad[0:rr, :] = rg[0, 0, 0].astype(F32)
+    for j in range(blocks):
+        route_out[j] = pad[:, j * 128 : (j + 1) * 128].astype(BF16)
+
+    pl.semaphore_wait(barrier, n - 1 + m - 1)
+
+    def remote(src, dst, send, recv, dp, tensor):
+        return pltpu.make_async_remote_copy(
+            src_ref=src,
+            dst_ref=dst,
+            send_sem=send,
+            recv_sem=recv,
+            device_id=(dp, tensor),
+            device_id_type=MESH,
+        )
+
+    sends = []
+
+    order = [(p, r, h) for p in range(len(pieces)) for h in range(2) for r in range(2)]
+
+    def rs_copy(s, p, r, h):
+        e_i, off, cols = pieces[p]
+        lane = slice(off, off + cols)
+        if s == 1:
+            owner = at_pos(pos + sign[r] * length[r][h])
+            src = (
+                ag.at[0, 0, row0(owner, h), :]
+                if e_i is None
+                else eg.at[0, 0, e_i, row0(owner, h), :]
+            )
+            dst = raw_in.at[r, h, :, lane]
+        else:
+            src = stage.at[r, h, :, lane] if s == 2 else sum_in.at[r, h, s - 3, :, lane]
+            dst = sum_in.at[r, h, s - 2, :, lane]
+        return remote(src, dst, rs_send.at[s - 1, p, r, h], rs_recv.at[s - 1, p, r, h], peers[r], t)
+
+    def for_tiles(cols, body):
+        wide = cols // WIDE
+
+        def step(i, carry):
+            body(pl.multiple_of((i // wide) * 16, 16), pl.multiple_of((i % wide) * WIDE, WIDE))
+            return carry
+
+        lax.fori_loop(0, (hr // 16) * wide, step, 0)
+
+    def own(p, owner, h, r0, c0):
+        e_i = pieces[p][0]
+        rws = pl.ds(pl.multiple_of(owner * rows + h * hr + r0, 16), 16)
+        cls = pl.ds(c0, WIDE)
+        return (ga[rws, cls] if e_i is None else ge[e_i, rws, cls]).astype(F32)
+
+    for item in order:
+        c = rs_copy(1, *item)
+        c.start()
+        sends.append(c)
+
+    def route_copy(k):
+        to = (d + k) % n
+        src = route_out.at[(to * m * own_cols) // 128]
+        return remote(src, route_in.at[k], route_sem.at[0, k], route_sem.at[1, k], to, t)
+
+    for k in range(1, n):
+        c = route_copy(k)
+        c.start()
+        sends.append(c)
+    for c in loads:
+        c.wait()
+    squares[...] = jnp.zeros_like(squares)
+
+    def route_first():
+        total = route_out[(d * m * own_cols) // 128].astype(F32)
+        for k in range(1, n):
+            route_copy(k).wait_recv()
+            total = total + route_in[k].astype(F32)
+        route_t[0] = total
+        for k in range(1, m):
+            c = route_second(k)
+            c.start()
+            sends.append(c)
+
+    def route_second(k):
+        return remote(
+            route_t.at[0],
+            route_t.at[k],
+            route_sem.at[2, k],
+            route_sem.at[3, k],
+            d,
+            (t + k) % m,
+        )
+
+    for s in range(1, half_n + 1):
+        for p, r, h in order:
+            if s > length[r][h]:
+                continue
+            e_i, off, cols = pieces[p]
+            rs_copy(s, p, r, h).wait_recv()
+            last = s == length[r][h]
+            owner = at_pos(pos + sign[r] * (length[r][h] - s))
+
+            def add(r0, c0, s=s, p=p, r=r, h=h, off=off, last=last, owner=owner):
+                rws = pl.ds(r0, 16)
+                cls = pl.ds(pl.multiple_of(off + c0, WIDE), WIDE)
+                if s == 1:
+                    got = raw_in[r, h, rws, cls].astype(F32)
+                else:
+                    got = sum_in[r, h, s - 2, rws, cls]
+                if last and s == half_n:
+                    total = gsum[h, rws, cls] + got
+                    gsum[h, rws, cls] = total
+                    sq = total * total
+                    sq = sq[0:8] + sq[8:16]
+                    acc = squares[...]
+                    for b in range(0, WIDE, 128):
+                        acc = acc + sq[:, b : b + 128]
+                    squares[...] = acc
+                    return
+                total = own(p, owner, h, r0, c0) + got
+                if last:
+                    gsum[h, rws, cls] = total
+                elif s == 1:
+                    stage[r, h, rws, cls] = total
+                else:
+                    sum_in[r, h, s - 2, rws, cls] = total
+
+            for_tiles(cols, add)
+            if not last:
+                c = rs_copy(s + 1, p, r, h)
+                c.start()
+                sends.append(c)
+        if s == 1:
+            route_first()
+
+        if s == half_n - 1:
+            block = route_t[0]
+            for k in range(1, m):
+                route_second(k).wait_recv()
+                block = block + route_t[k]
+            place = (d * m + t) % per_block
+            route_sum = jnp.zeros((pad.shape[0], own_cols), F32)
+            for b in range(per_block):
+                hit = (place == b).astype(F32)
+                route_sum = route_sum + hit * block[:, b * own_cols : (b + 1) * own_cols]
+            route_sq = jnp.sum(route_sum * route_sum, keepdims=True)
+
+    lane = lax.broadcasted_iota(jnp.int32, (8, 128), 1)
+    sub = lax.broadcasted_iota(jnp.int32, (8, 128), 0)
+    first = ((lane == 0) & (sub == 0)).astype(F32)
+    norm_t[t] = squares[...] + first * route_sq
+
+    def norm_copy(level, k):
+        if level == 0:
+            buf, who, dp, tensor = norm_t, t, d, (t + k) % m
+        else:
+            buf, who, dp, tensor = norm_d, d, (d + k) % n, t
+        return remote(buf.at[who], buf.at[who], norm_sem.at[level, 0, k], norm_sem.at[level, 1, k], dp, tensor)
+
+    def norm_wait(level, k):
+        if level == 0:
+            buf, who = norm_t, (t + m - k) % m
+        else:
+            buf, who = norm_d, (d + n - k) % n
+        remote(buf.at[who], buf.at[who], norm_sem.at[level, 0, k], norm_sem.at[level, 1, k], d, t).wait_recv()
+
+    for k in range(1, m):
+        c = norm_copy(0, k)
+        c.start()
+        sends.append(c)
+    for c in state_loads:
+        c.wait()
+    for k in range(1, m):
+        norm_wait(0, k)
+    total = norm_t[0]
+    for k in range(1, m):
+        total = total + norm_t[k]
+    norm_d[d] = total
+    for k in range(1, n):
+        c = norm_copy(1, k)
+        c.start()
+        sends.append(c)
+    steps = jnp.full((1, 1), step_ref[0], jnp.int32)
+    first_fix = 1.0 - power(BETA_ONE, steps)
+    second_fix = 1.0 - power(BETA_TWO, steps)
+    rate = rate_ref[0]
+    for k in range(1, n):
+        norm_wait(1, k)
+    total = norm_d[0]
+    for k in range(1, n):
+        total = total + norm_d[k]
+    grad_norm = jnp.sqrt(jnp.sum(total, keepdims=True))
+    level = jnp.full((1, 1), level_ref[0], F32)
+    clip = jnp.minimum(1.0, level * F32(np.sqrt(np.float32(PARAMS))) / (grad_norm + 1e-06))
+
+    def renew(total, master, first_moment, second_moment, mask):
+        grad = clip * total
+        momentum = BETA_ONE * first_moment + (1.0 - BETA_ONE) * grad
+        variance = BETA_TWO * second_moment + (1.0 - BETA_TWO) * grad * grad
+        update = (
+            momentum / first_fix / (jnp.sqrt(variance / second_fix) + EPSILON)
+            + DECAY * mask * master
+        )
+        return master - rate * update, momentum, variance
+
+    def out_rows(p, owner, h):
+        e_i = pieces[p][0]
+        return o_as.at[row0(owner, h), :] if e_i is None else o_es.at[e_i, row0(owner, h), :]
+
+    def ag_copy(s, p, r, h):
+        e_i, off, cols = pieces[p]
+        owner = at_pos(pos - sign[r] * (s - 1))
+        dst = out_rows(p, owner, h)
+        src = served.at[h, :, off : off + cols] if s == 1 else dst
+        return remote(src, dst, ag_send.at[s - 1, p, r, h], ag_recv.at[s - 1, p, r, h], peers[r], t)
+
+    def ag_wait(s, p, r, h):
+        owner = at_pos(pos - sign[r] * s)
+        dst = out_rows(p, owner, h)
+        remote(dst, dst, ag_send.at[s - 1, p, r, h], ag_recv.at[s - 1, p, r, h], peers[r], t).wait_recv()
+
+    outs = []
+    k = 0
+    for p in range(len(pieces)):
+        e_i, off, cols = pieces[p]
+        for h in range(2):
+
+            def update(r0, c0, h=h, off=off):
+                cls = pl.ds(pl.multiple_of(off + c0, WIDE), WIDE)
+                rws = pl.ds(pl.multiple_of(h * hr + r0, 16), 16)
+                w, mom, var = renew(
+                    gsum[h, pl.ds(r0, 16), cls],
+                    st[0, rws, cls],
+                    st[1, rws, cls],
+                    st[2, rws, cls],
+                    1.0,
+                )
+                st[0, rws, cls] = w
+                st[1, rws, cls] = mom
+                st[2, rws, cls] = var
+                served[h, pl.ds(r0, 16), cls] = w.astype(BF16)
+
+            for_tiles(cols, update)
+            for r in range(2):
+                c = ag_copy(1, p, r, h)
+                c.start()
+                sends.append(c)
+            c = pltpu.make_async_copy(
+                served.at[h, :, off : off + cols], out_rows(p, d, h), out_sem.at[k]
+            )
+            k += 1
+            c.start()
+            outs.append(c)
+        for which, (a, e) in enumerate(((o_am, o_em), (o_af, o_ef), (o_av, o_ev))):
+            dst = a if e_i is None else e.at[e_i]
+            c = pltpu.make_async_copy(st.at[which, :, off : off + cols], dst, out_sem.at[k])
+            k += 1
+            c.start()
+            outs.append(c)
+
+    route_sum = route_sum[0:rr]
+    row_index = lax.broadcasted_iota(jnp.int32, (rr, own_cols), 0)
+    mask = (row_index < EXPERTS).astype(F32)
+    w, mom, var = renew(route_sum, rm[...], rf[...], rv[...], mask)
+    o_rm[...] = w
+    o_rf[...] = mom
+    o_rv[...] = var
+    pad[0:rr, 0:128] = jnp.concatenate(
+        [(place == b).astype(F32) * w for b in range(per_block)], axis=1
+    )
+    pad[rr:, 0:128] = jnp.zeros((pad.shape[0] - rr, 128), F32)
+    serve_t[0] = pad[:, 0:128].astype(BF16)
+
+    def serve_copy(k):
+        return remote(
+            serve_t.at[0], serve_t.at[k], route_sem.at[4, k], route_sem.at[5, k], d, (t + k) % m
+        )
+
+    def spread_copy(k):
+        return remote(
+            serve_d.at[d], serve_d.at[d], route_sem.at[6, k], route_sem.at[7, k], (d + k) % n, t
+        )
+
+    def spread_wait(k):
+        who = (d + n - k) % n
+        remote(
+            serve_d.at[who], serve_d.at[who], route_sem.at[6, k], route_sem.at[7, k], d, t
+        ).wait_recv()
+
+    for k in range(1, m):
+        c = serve_copy(k)
+        c.start()
+        sends.append(c)
+
+    for s in range(1, half_n + 1):
+        for p, r, h in order:
+            if s > length[r][h]:
+                continue
+            ag_wait(s, p, r, h)
+            if s < length[r][h]:
+                c = ag_copy(s + 1, p, r, h)
+                c.start()
+                sends.append(c)
+        if s == 1:
+            block = serve_t[0].astype(F32)
+            for k in range(1, m):
+                serve_copy(k).wait_recv()
+                block = block + serve_t[k].astype(F32)
+            serve_d[d] = block.astype(BF16)
+            for k in range(1, n):
+                c = spread_copy(k)
+                c.start()
+                sends.append(c)
+        if s == half_n - 1:
+            for k in range(1, n):
+                spread_wait(k)
+            each = n // blocks
+            parts = []
+            for j in range(blocks):
+                block = serve_d[j * each].astype(F32)
+                for b in range(1, each):
+                    block = block + serve_d[j * each + b].astype(F32)
+                parts.append(block[0:rr])
+            o_rs[...] = jnp.concatenate(parts, axis=1).astype(BF16)
+
+    for c in outs:
+        c.wait()
+    for c in sends:
+        c.wait_send()
+
+
+def ring_local(mesh, *args):
+    n, m = mesh.shape["dp"], mesh.shape["tensor"]
+    (ag, eg, rg, am, af, av, em, ef, ev, rm, rf, rv, step, rate, level) = args
+    rows, wa = am.shape
+    ne, _, we = em.shape
+    rr, rc = rg.shape[-2:]
+    fits = (
+        n % 2 == 0
+        and n >= 4
+        and rows % 32 == 0
+        and wa % WIDE == 0
+        and we % WIDE == 0
+        and ag.shape[1] == 1
+        and eg.shape[1] == 1
+        and rg.shape[2] == 1
+        and rc % 128 == 0
+        and 128 % (rc // (n * m)) == 0
+        and n % (rc // 128) == 0
+    )
+    if not fits:
+        return local(*args)
+    width = wa + ne * we
+    half_n = n // 2
+    hr = rows // 2
+    pr = -(-rr // 16) * 16
+    np_ = 1 + ne
+    dma = pltpu.SemaphoreType.DMA
+    hbm = pl.BlockSpec(memory_space=pl.ANY)
+    vmem = pl.BlockSpec(memory_space=pltpu.VMEM)
+    smem = pl.BlockSpec(memory_space=pltpu.SMEM)
+    sds = jax.ShapeDtypeStruct
+    served_a = sds((n * rows, wa), BF16)
+    served_e = sds((ne, n * rows, we), BF16)
+    like = lambda a: sds(a.shape, a.dtype)
+    return pl.pallas_call(
+        functools.partial(ring_kernel, n, m),
+        out_shape=(
+            like(am),
+            like(am),
+            like(am),
+            served_a,
+            like(em),
+            like(em),
+            like(em),
+            served_e,
+            like(rm),
+            like(rm),
+            like(rm),
+            sds((rr, rc), BF16),
+        ),
+        in_specs=[hbm, hbm, vmem] + [hbm] * 6 + [vmem] * 3 + [smem] * 3,
+        out_specs=(hbm,) * 8 + (vmem,) * 4,
+        scratch_shapes=[
+            pltpu.VMEM((n * rows, wa), BF16),
+            pltpu.VMEM((ne, n * rows, we), BF16),
+            pltpu.VMEM((3, rows, width), F32),
+            pltpu.VMEM((2, 2, hr, width), BF16),
+            pltpu.VMEM((2, 2, half_n - 1, hr, width), F32),
+            pltpu.VMEM((2, 2, hr, width), F32),
+            pltpu.VMEM((2, hr, width), F32),
+            pltpu.VMEM((2, hr, width), BF16),
+            pltpu.VMEM((8, 128), F32),
+            pltpu.VMEM((m, 8, 128), F32),
+            pltpu.VMEM((n, 8, 128), F32),
+            pltpu.VMEM((pr, rc), F32),
+            pltpu.VMEM((rc // 128, pr, 128), BF16),
+            pltpu.VMEM((n, pr, 128), BF16),
+            pltpu.VMEM((m, pr, 128), F32),
+            pltpu.VMEM((m, pr, 128), BF16),
+            pltpu.VMEM((n, pr, 128), BF16),
+            dma((2 + 3 * np_,)),
+            dma((half_n, np_, 2, 2)),
+            dma((half_n, np_, 2, 2)),
+            dma((half_n, np_, 2, 2)),
+            dma((half_n, np_, 2, 2)),
+            dma((2, 2, max(n, m))),
+            dma((8, max(n, m))),
+            dma((5 * np_,)),
+        ],
+        compiler_params=pltpu.CompilerParams(
+            collective_id=3, has_side_effects=True, vmem_limit_bytes=40 * 2**20
+        ),
+    )(*args)
+
+
 def solution(mesh):
     in_specs = (
         P("dp", None, None, "tensor"),
@@ -161,4 +697,5 @@
         P(None, ("dp", "tensor")),
         P(),
     )
-    return jax.shard_map(local, mesh=mesh, in_specs=in_specs, out_specs=out_specs, check_vma=False)
+    body = functools.partial(ring_local, mesh)
+    return jax.shard_map(body, mesh=mesh, in_specs=in_specs, out_specs=out_specs, check_vma=False)

time: 436 us -> 125 us (0.29)
  waiting for transfers between devices: 283 us -> 0 us
  blocking collectives: 113 us -> 0 us
  Pallas kernels: 0 us -> 89.6 us
  local copies, waits for them, and re-layouts: 5.74 us -> 31.9 us
  between operations: 19.4 us -> 2.63 us
  other arithmetic: 13.9 us -> 0 us
    reduce_scatter x3 -> x0, waiting for transfers between devices: 283 us -> none  [the longest x1 131 us: local(): lax.psum_scatter(routing_local, ('dp', 'tensor'), scatter_dimension=1, ti...]
    pallas_call x0 -> x1, Pallas kernels: none -> 89.6 us  [ring_local(): pl.pallas_call(functools.partial(ring_kernel, n, m), out_shape=(like(am),...]
    all_gather x2 -> x0, blocking collectives: 72.9 us -> none  [the longest x1 40.3 us: local(): lax.all_gather(routing_out[3], ('dp', 'tensor'), axis=1, tiled=True)]
    psum x1 -> x0, blocking collectives: 40.3 us -> none  [local(): lax.psum((jnp.sum(attention_sum * attention_sum), expert_squares, jnp.sum...]
    unnamed x28 -> x52, local copies, waits for them, and re-layouts: 5.74 us -> 27.7 us
    convert_element_type x6 -> x0, other arithmetic: 9.37 us -> none  [the longest x3 5.27 us: micro_total(): blocks[0].astype(jnp.float32)]
    reduce_sum x3 -> x0, other arithmetic: 4.55 us -> none  [the longest x1 1.7 us: local(): jnp.sum(piece * piece)]
  transfers between devices with their start and end apart: 4 -> 0, of which waited for: 3 -> 0; matrix products, arithmetic and copies ran while one was open for 2% -> 0% of each run, Pallas kernels for 0% -> 0%
where the time goes in v1:
time: 125 us; the launch traced here: 124 us
  Pallas kernels  89.6 us (72%)
  local copies, waits for them, and re-layouts  31.9 us (26%)
  between operations  2.63 us (2%)
    pallas_call x1, Pallas kernels, ring_local(): pl.pallas_call(functools.partial(ring_kernel, n, m), out_shape=(like(am),...  89.6 us
    unnamed x52, local copies, waits for them, and re-layouts  27.7 us
    pallas_call x3, local copies, waits for them, and re-layouts, ring_local(): pl.pallas_call(functools.partial(ring_kernel, n, m), out_shape=(like(am),...  4.19 us

profile of v1, /device:TPU:0, one launch (start us, length us, event | category | flops | bytes accessed | tf_op | source)
XLA Modules:
  0.0 124.2 jit_solution(11776844283771259724)
XLA Ops:
  2.6 1.4 %copy.27.rm = f32[36,16]{1,0:T(8,128)} copy(f32[36,16]{0,1:T(8,128)} %param.24) | data formatting | bytes 4608 | tf_op args[9]
  4.0 1.4 %copy.28.rf = f32[36,16]{1,0:T(8,128)} copy(f32[36,16]{0,1:T(8,128)} %param.25) | data formatting | bytes 4608 | tf_op args[10]
  5.4 1.4 %copy.29.rv = f32[36,16]{1,0:T(8,128)} copy(f32[36,16]{0,1:T(8,128)} %param.26) | data formatting | bytes 4608 | tf_op args[11]
  6.7 0.0 copy-start
  6.7 1.6 %copy-done = bf16[1,1,2,512,1024]{4,3,2,1,0:T(8,128)(2,1)S(1)} copy-done((bf16[1,1,2,512,1024]{4,3,2,1,0:T(8,128)(2,1)S(1)}, bf16[1,1,2,512,1024]{4,3,2,1,0:T(8,128)(2,1)}, u32[]{:S(2)}) %copy-start) | copy-done | bytes 2097176
  8.3 0.0 copy-start.1
  8.3 1.0 copy-done.1
  9.4 0.0 copy-start.2
  9.4 1.0 copy-done.2
  10.4 0.0 copy-start.3
  10.4 1.0 copy-done.3
  11.5 0.0 copy-start.4
  11.5 1.0 copy-done.4
  12.5 0.0 copy-start.8
  12.5 0.9 copy-done.8
  13.4 0.9 copy-done.9
  14.3 0.0 copy-start.10
  14.3 0.9 copy-done.10
  15.2 0.0 copy-start.11
  15.2 0.7 copy-done.11
  15.9 0.0 copy-start.12
  15.9 0.7 copy-done.12
  16.7 0.0 copy-start.13
  16.7 0.7 copy-done.13
  17.4 0.0 copy-start.14
  17.4 0.8 copy-done.14
  18.2 89.6 %shard_map.238 = (f32[64,512]{1,0:T(8,128)S(1)}, f32[64,512]{1,0:T(8,128)S(1)}, f32[64,512]{1,0:T(8,128)S(1)}, bf16[512,512]{1,0:T(8,128)(2,1)S(1)}, f32[2,64,10...) custom-call(bf16[1,1,512,512]{3,2,1,0:T(8,128)(2,1)S(1)} %copy-done., ...), custom_call_target="tpu_custom_call" | custom-call | tf_op jit(solution)/shard_map/pallas_call | solution.py:617
  107.8 0.0 copy-start.5
  107.8 0.8 copy-done.5
  108.6 0.8 copy-done.7
  109.4 0.6 copy-done.15
  110.0 0.6 copy-done.17
  110.6 0.6 copy-done.18
  111.2 0.6 copy-done.19
  111.8 1.4 %copy.30 = f32[36,16]{0,1:T(8,128)} copy(f32[36,16]{1,0:T(8,128)} %copy-done.19) | data formatting | bytes 4608 | tf_op jit(solution)/shard_map/pallas_call | solution.py:617
  113.2 1.4 %copy.31 = f32[36,16]{0,1:T(8,128)} copy(f32[36,16]{1,0:T(8,128)} %copy-done.18) | data formatting | bytes 4608 | tf_op jit(solution)/shard_map/pallas_call | solution.py:617
  114.6 1.4 %copy.32 = f32[36,16]{0,1:T(8,128)} copy(f32[36,16]{1,0:T(8,128)} %copy-done.17) | data formatting | bytes 4608 | tf_op jit(solution)/shard_map/pallas_call | solution.py:617
  116.0 0.7 copy.45
  116.6 0.7 copy.46
  117.3 0.7 copy.47
  118.0 1.9 %copy.48 = bf16[512,512]{1,0:T(8,128)(2,1)} copy(bf16[512,512]{1,0:T(8,128)(2,1)} %copy-done.7) | data formatting | bytes 1048576
  119.8 0.0 copy-done.6
  119.8 0.8 copy.49
  120.6 0.8 copy.50
  121.4 0.8 copy.51
  122.2 1.3 %copy.52 = bf16[2,512,1024]{2,1,0:T(8,128)(2,1)} copy(bf16[2,512,1024]{2,1,0:T(8,128)(2,1)S(1)} %get-tuple-element.43) | data formatting | bytes 4194304
  123.5 0.0 copy-done.16
  123.5 0.6 copy.53
  (8 shorter events, 0.0 us)
Async XLA Ops:
  6.7 1.6 %copy-start = (bf16[1,1,2,512,1024]{4,3,2,1,0:T(8,128)(2,1)S(1)}, bf16[1,1,2,512,1024]{4,3,2,1,0:T(8,128)(2,1)}, u32[]{:S(2)}) copy-start(bf16[1,1,2,512,1024]{4,3,2,1,0:T(8,128)(2,1)} %eg.1) | copy-start | bytes 6291460
  8.3 1.0 copy-start.1
  9.4 1.0 copy-start.2
  10.4 1.0 copy-start.3
  11.5 1.0 copy-start.4
  12.5 0.9 copy-start.8
  13.4 0.9 copy-start.9
  14.3 0.9 copy-start.10
  15.2 0.7 copy-start.11
  15.9 0.7 copy-start.12
  16.7 0.7 copy-start.13
  17.4 0.8 copy-start.14
  107.8 0.8 copy-start.5
  108.6 0.8 copy-start.7
  109.4 0.6 copy-start.15
  110.0 0.6 copy-start.17
  110.6 0.6 copy-start.18
  111.2 0.6 copy-start.19
  116.0 3.8 %copy-start.6 = (f32[2,64,1024]{2,1,0:T(8,128)S(1)}, f32[2,64,1024]{2,1,0:T(8,128)}, u32[]{:S(2)}) copy-start(f32[2,64,1024]{2,1,0:T(8,128)} %copy-done.5) | copy-start | bytes 1572868
  122.2 1.3 %copy-start.16 = (bf16[36,512]{1,0:T(8,128)(2,1)S(1)}, bf16[36,512]{1,0:T(8,128)(2,1)}, u32[]{:S(2)}) copy-start(bf16[36,512]{1,0:T(8,128)(2,1)} %copy-done.15) | copy-start | bytes 110596

commit v2 on v1

--- a/solution.py
+++ b/solution.py
@@ -189,6 +189,7 @@
     norm_t,
     norm_d,
     pad,
+    square,
     route_out,
     route_in,
     route_t,
@@ -320,6 +321,7 @@
     for c in loads:
         c.wait()
     squares[...] = jnp.zeros_like(squares)
+    square[...] = jnp.zeros_like(square)
 
     def route_first():
         total = route_out[(d * m * own_cols) // 128].astype(F32)
@@ -509,15 +511,18 @@
             c.start()
             outs.append(c)
 
-    route_sum = route_sum[0:rr]
-    row_index = lax.broadcasted_iota(jnp.int32, (rr, own_cols), 0)
+    square[0 : pad.shape[0], 0:own_cols] = route_sum
+    route_sum = jnp.transpose(square[...])[0:own_cols, 0:rr]
+    row_index = lax.broadcasted_iota(jnp.int32, (own_cols, rr), 1)
     mask = (row_index < EXPERTS).astype(F32)
     w, mom, var = renew(route_sum, rm[...], rf[...], rv[...], mask)
+    square[0:own_cols, 0:rr] = w
+    w_rows = jnp.transpose(square[...])[0:rr, 0:own_cols]
     o_rm[...] = w
     o_rf[...] = mom
     o_rv[...] = var
     pad[0:rr, 0:128] = jnp.concatenate(
-        [(place == b).astype(F32) * w for b in range(per_block)], axis=1
+        [(place == b).astype(F32) * w_rows for b in range(per_block)], axis=1
     )
     pad[rr:, 0:128] = jnp.zeros((pad.shape[0] - rr, 128), F32)
     serve_t[0] = pad[:, 0:128].astype(BF16)
@@ -580,6 +585,19 @@
         c.wait_send()
 
 
+def place_kernel(count, *refs):
+    ins, outs, sem = refs[:count], refs[count : 2 * count], refs[2 * count]
+    copies = [
+        pltpu.make_async_copy(src, dst, sem.at[k])
+        for k, (src, dst) in enumerate(zip(ins[:-1], outs[:-1]))
+    ]
+    for c in copies:
+        c.start()
+    outs[-1][...] = ins[-1][...]
+    for c in copies:
+        c.wait()
+
+
 def ring_local(mesh, *args):
     n, m = mesh.shape["dp"], mesh.shape["tensor"]
     (ag, eg, rg, am, af, av, em, ef, ev, rm, rf, rv, step, rate, level) = args
@@ -597,6 +615,7 @@
         and rg.shape[2] == 1
         and rc % 128 == 0
         and 128 % (rc // (n * m)) == 0
+        and rr <= 112
         and n % (rc // 128) == 0
     )
     if not fits:
@@ -607,14 +626,16 @@
     pr = -(-rr // 16) * 16
     np_ = 1 + ne
     dma = pltpu.SemaphoreType.DMA
-    hbm = pl.BlockSpec(memory_space=pl.ANY)
+    hbm = pl.BlockSpec(memory_space=pltpu.HBM)
+    anywhere = pl.BlockSpec(memory_space=pl.ANY)
     vmem = pl.BlockSpec(memory_space=pltpu.VMEM)
     smem = pl.BlockSpec(memory_space=pltpu.SMEM)
     sds = jax.ShapeDtypeStruct
     served_a = sds((n * rows, wa), BF16)
     served_e = sds((ne, n * rows, we), BF16)
     like = lambda a: sds(a.shape, a.dtype)
-    return pl.pallas_call(
+    rm, rf, rv = rm.T, rf.T, rv.T
+    results = pl.pallas_call(
         functools.partial(ring_kernel, n, m),
         out_shape=(
             like(am),
@@ -631,7 +652,7 @@
             sds((rr, rc), BF16),
         ),
         in_specs=[hbm, hbm, vmem] + [hbm] * 6 + [vmem] * 3 + [smem] * 3,
-        out_specs=(hbm,) * 8 + (vmem,) * 4,
+        out_specs=(anywhere,) * 8 + (vmem,) * 4,
         scratch_shapes=[
             pltpu.VMEM((n * rows, wa), BF16),
             pltpu.VMEM((ne, n * rows, we), BF16),
@@ -645,6 +666,7 @@
             pltpu.VMEM((m, 8, 128), F32),
             pltpu.VMEM((n, 8, 128), F32),
             pltpu.VMEM((pr, rc), F32),
+            pltpu.VMEM((128, 128), F32),
             pltpu.VMEM((rc // 128, pr, 128), BF16),
             pltpu.VMEM((n, pr, 128), BF16),
             pltpu.VMEM((m, pr, 128), F32),
@@ -660,9 +682,19 @@
             dma((5 * np_,)),
         ],
         compiler_params=pltpu.CompilerParams(
-            collective_id=3, has_side_effects=True, vmem_limit_bytes=40 * 2**20
+            collective_id=3, has_side_effects=True, vmem_limit_bytes=62 * 2**20
         ),
-    )(*args)
+    )(ag, eg, rg, am, af, av, em, ef, ev, rm, rf, rv, step, rate, level)
+    count = len(results)
+    final = pl.pallas_call(
+        functools.partial(place_kernel, count),
+        out_shape=tuple(like(a) for a in results),
+        in_specs=[anywhere] * (count - 1) + [vmem],
+        out_specs=(hbm,) * (count - 1) + (vmem,),
+        scratch_shapes=[dma((count - 1,))],
+        compiler_params=pltpu.CompilerParams(vmem_limit_bytes=62 * 2**20),
+    )(*results)
+    return final[:8] + (final[8].T, final[9].T, final[10].T, final[11])
 
 
 def solution(mesh):

time: 125 us -> 236 us (1.89)
  Pallas kernels: 89.6 us -> 234 us
  local copies, waits for them, and re-layouts: 31.9 us -> 0 us
    pallas_call x0 -> x1, Pallas kernels: none -> 142 us  [ring_local(): pl.pallas_call(functools.partial(place_kernel, count), out_shape=tuple((l...]
    unnamed x52 -> x0, local copies, waits for them, and re-layouts: 27.7 us -> none
    pallas_call x3 -> x0, local copies, waits for them, and re-layouts: 4.19 us -> none  [ring_local(): pl.pallas_call(functools.partial(ring_kernel, n, m), out_shape=(like(am),...]
where the time goes in v2:
time: 236 us
  Pallas kernels  234 us (99%)
  between operations  2.59 us (1%)
    pallas_call x1, Pallas kernels, ring_local(): pl.pallas_call(functools.partial(place_kernel, count), out_shape=tuple((l...  142 us
    pallas_call x1, Pallas kernels, ring_local(): pl.pallas_call(functools.partial(ring_kernel, n, m), out_shape=(like(am),...  91.3 us

profile of v2, /device:TPU:0, one launch (start us, length us, event | category | flops | bytes accessed | tf_op | source)
XLA Modules:
  0.0 236.2 jit_solution(10134867527568470250)
XLA Ops:
  2.6 91.3 %shard_map.238 = (f32[64,512]{1,0:T(8,128)}, f32[64,512]{1,0:T(8,128)}, f32[64,512]{1,0:T(8,128)}, bf16[512,512]{1,0:T(8,128)(2,1)}, f32[2,64,1024]{2,1,0:T(8,12...) custom-call(bf16[1,1,512,512]{3,2,1,0:T(8,128)(2,1)} %ag.1, ...), custom_call_target="tpu_custom_call" | custom-call | tf_op jit(solution)/shard_map/pallas_call | solution.py:638
  93.9 142.3 %shard_map.239 = (f32[64,512]{1,0:T(8,128)}, f32[64,512]{1,0:T(8,128)}, f32[64,512]{1,0:T(8,128)}, bf16[512,512]{1,0:T(8,128)(2,1)}, f32[2,64,1024]{2,1,0:T(8,12...) custom-call(f32[64,512]{1,0:T(8,128)} %get-tuple-element.36.refs_0_,, ...), custom_call_target="tpu_custom_call" | custom-call | tf_op jit(solution)/shard_map/pallas_call | solution.py:689

commit v3 on v2

--- a/solution.py
+++ b/solution.py
@@ -586,15 +586,21 @@
 
 
 def place_kernel(count, *refs):
-    ins, outs, sem = refs[:count], refs[count : 2 * count], refs[2 * count]
-    copies = [
-        pltpu.make_async_copy(src, dst, sem.at[k])
-        for k, (src, dst) in enumerate(zip(ins[:-1], outs[:-1]))
+    ins, outs = refs[:count], refs[count : 2 * count]
+    held, sem = refs[2 * count : 3 * count - 1], refs[3 * count - 1]
+    arrive = [
+        pltpu.make_async_copy(ins[k], held[k], sem.at[0, k]) for k in range(count - 1)
     ]
-    for c in copies:
+    leave = [
+        pltpu.make_async_copy(held[k], outs[k], sem.at[1, k]) for k in range(count - 1)
+    ]
+    for c in arrive:
         c.start()
     outs[-1][...] = ins[-1][...]
-    for c in copies:
+    for a, b in zip(arrive, leave):
+        a.wait()
+        b.start()
+    for c in leave:
         c.wait()
 
 
@@ -691,7 +697,7 @@
         out_shape=tuple(like(a) for a in results),
         in_specs=[anywhere] * (count - 1) + [vmem],
         out_specs=(hbm,) * (count - 1) + (vmem,),
-        scratch_shapes=[dma((count - 1,))],
+        scratch_shapes=[pltpu.VMEM(a.shape, a.dtype) for a in results[:-1]] + [dma((2, count - 1))],
         compiler_params=pltpu.CompilerParams(vmem_limit_bytes=62 * 2**20),
     )(*results)
     return final[:8] + (final[8].T, final[9].T, final[10].T, final[11])

time: 236 us -> 100 us (0.42)
  Pallas kernels: 234 us -> 97.6 us
    pallas_call x1, Pallas kernels: 142 us -> 6.26 us  [ring_local(): pl.pallas_call(functools.partial(place_kernel, count), out_shape=tuple((l...]
where the time goes in v3:
time: 100 us
  Pallas kernels  97.6 us (98%)
  between operations  2.59 us (3%)
    pallas_call x1, Pallas kernels, ring_local(): pl.pallas_call(functools.partial(ring_kernel, n, m), out_shape=(like(am),...  91.3 us
    pallas_call x1, Pallas kernels, ring_local(): pl.pallas_call(functools.partial(place_kernel, count), out_shape=tuple((l...  6.26 us

profile of v3, /device:TPU:0, one launch (start us, length us, event | category | flops | bytes accessed | tf_op | source)
XLA Modules:
  0.0 100.2 jit_solution(13509587027440492909)
XLA Ops:
  2.6 91.3 %shard_map.238 = (f32[64,512]{1,0:T(8,128)}, f32[64,512]{1,0:T(8,128)}, f32[64,512]{1,0:T(8,128)}, bf16[512,512]{1,0:T(8,128)(2,1)}, f32[2,64,1024]{2,1,0:T(8,12...) custom-call(bf16[1,1,512,512]{3,2,1,0:T(8,128)(2,1)} %ag.1, ...), custom_call_target="tpu_custom_call" | custom-call | tf_op jit(solution)/shard_map/pallas_call | solution.py:644
  93.9 6.3 %shard_map.239 = (f32[64,512]{1,0:T(8,128)}, f32[64,512]{1,0:T(8,128)}, f32[64,512]{1,0:T(8,128)}, bf16[512,512]{1,0:T(8,128)(2,1)}, f32[2,64,1024]{2,1,0:T(8,12...) custom-call(f32[64,512]{1,0:T(8,128)} %get-tuple-element.36.refs_0_,, ...), custom_call_target="tpu_custom_call" | custom-call | tf_op jit(solution)/shard_map/pallas_call | solution.py:695
